TPU v7x, 32 devices: a whole 2x2x4 slice. The times are simulated.
32 devices in a mesh: hid: 8 (over y, x, core), wid: 4 (over z).
Axes of the slice: x: 2, y: 2, z: 4, core: 2. Of those that a mesh axis runs over, the one named last changes fastest.
Arguments:
- tokens: bfloat16 [32, 16384], P('hid', 'wid'), may hold values from -6 to 6
- gate_weight: bfloat16 [16384, 26624], P('wid', 'hid'), may hold values from -0.046875 to 0.046875
- up_weight: bfloat16 [16384, 26624], P('wid', 'hid'), may hold values from -0.046875 to 0.046875
- down_weight: bfloat16 [26624, 16384], P('hid', 'wid'), may hold values from -0.0390625 to 0.0390625
Outputs:
- stream: bfloat16 [32, 16384], P('hid', 'wid')
All inputs are finite; a program needn't handle non-finite values.
Results may differ from a plain program's by a relative error of at most 0.035.
Values may be sent and summed in bfloat16 or wider, within the bound.
A program may use at most 128 MiB of HBM per device.

v0:
```python
import jax
import jax.numpy as jnp
from jax import lax
from jax.sharding import PartitionSpec as P

STEPS = 2


def activate(partial_value):
    totals = lax.psum(partial_value.astype(jnp.bfloat16), "wid").astype(jnp.float32)
    return (jax.nn.silu(totals[:, 0]) * totals[:, 1]).astype(jnp.bfloat16)


def per_device(tokens, gate_weight, up_weight, down_weight):
    stream = tokens
    for repeat in range(STEPS):
        shard_rows = lax.all_gather(stream, "hid", axis=0, tiled=True)
        gate_part = jnp.dot(shard_rows, gate_weight, preferred_element_type=jnp.float32)
        up_part = jnp.dot(shard_rows, up_weight, preferred_element_type=jnp.float32)
        partial_value = jnp.stack([gate_part, up_part], axis=1)
        hidden = activate(partial_value)
        branch = lax.psum_scatter(
            jnp.dot(hidden, down_weight, preferred_element_type=jnp.float32),
            "hid",
            scatter_dimension=0,
            tiled=True,
        )
        stream = (stream.astype(jnp.float32) + branch).astype(jnp.bfloat16)
    return stream


def solution(mesh):
    in_specs = (P("hid", "wid"), P("wid", "hid"), P("wid", "hid"), P("hid", "wid"))
    out_specs = P("hid", "wid")
    return jax.shard_map(
        per_device, mesh=mesh, in_specs=in_specs, out_specs=out_specs, check_vma=False
    )
```

profile of v0, /device:TPU:0, one launch (start us, length us, event | category | flops | bytes accessed | tf_op | source)
XLA Modules:
  0.0 291.4 jit_solution(9883890441167134678)
XLA Ops:
  6.5 0.0 all-reduce.7.cloned.1.call-start
  6.5 11.0 %all-gather = bf16[8,4,4096]{2,1,0:T(4,128)(2,1)S(1)} all-gather(bf16[1,4,4096]{2,1,0:T(4,128)(2,1)} %bitcast.46), channel_id=1, replica_groups=mesh['hid'=8,'wid'=4] {'hid'}, dimensions={0}, use_global_device_ids=true | all-gather | bytes 294912 | tf_op jit(solution)/shard_map/all_gather | solution.py:17
  17.5 0.1 reshape.1
  17.6 11.2 %fusion.1 = bf16[32,1,3328]{2,0,1:T(8,128)(2,1)S(1)} fusion(bf16[32,4096]{1,0:T(8,128)(2,1)S(1)} %reshape.1, bf16[4096,3328]{1,0:T(8,128)(2,1)} %param.6), kind=kOutput, calls=%fused_computation.5 | convolution fusion | flops 872521728 | bytes 27738112 | tf_op jit(solution)/shard_map/dot_general | solution.py:19
  28.8 11.2 %fusion = bf16[32,1,3328]{2,0,1:T(8,128)(2,1)S(1)} fusion(bf16[32,4096]{1,0:T(8,128)(2,1)S(1)} %reshape.1, bf16[4096,3328]{1,0:T(8,128)(2,1)} %param.5), kind=kOutput, calls=%fused_computation.4 | convolution fusion | flops 872521728 | bytes 27738112 | tf_op jit(solution)/shard_map/dot_general | solution.py:18
  40.0 0.0 copy-start.1
  40.0 0.0 copy-start
  40.0 0.8 pad_maximum_fusion
  40.8 0.0 all-reduce.7.cloned.1.call-update
  40.9 0.0 all-reduce.11.cloned.1.call-start
  40.9 37.6 %all-reduce.7.cloned.1.call-done = bf16[32,2,3328]{2,0,1:T(8,128)(2,1)} async-done(((bf16[32,2,3328]{2,0,1:T(8,128)(2,1)}), bf16[32,2,3328]{2,0,1:T(8,128)(2,1)}) %all-reduce.7.cloned.1.call-update) | async-done | bytes 426000 | tf_op jit(solution)/shard_map/psum | solution.py:10
  78.5 1.1 convert_element_type.27
  79.6 12.0 %fusion.8 = f32[32,4096]{1,0:T(8,128)} fusion(bf16[3328,4096]{1,0:T(8,128)(2,1)} %param.7, f32[32,2,3328]{2,0,1:T(8,128)S(1)} %convert_element_type.27), kind=kOutput, calls=%fused_computation.18 | convolution fusion | flops 873054208 | bytes 28639232 | tf_op jit(solution)/shard_map/dot_general | solution.py:23
  91.6 0.0 all-reduce.11.cloned.1.call-update
  91.6 0.0 all-reduce.9.cloned.1.call-start
  91.7 0.0 copy-done.1
  91.7 0.6 dynamic-slice
  92.9 52.9 %all-reduce.11.cloned.1.call-done = f32[32,4096]{1,0:T(8,128)} async-done(((f32[32,4096]{1,0:T(8,128)}), f32[32,4096]{1,0:T(8,128)}) %all-reduce.11.cloned.1.call-update) | async-done | bytes 524304
  145.8 0.0 copy-done
  145.8 0.9 fusion.18
  146.7 8.6 %all-gather.1 = bf16[8,4,4096]{2,1,0:T(4,128)(2,1)S(1)} all-gather(bf16[1,4,4096]{2,1,0:T(4,128)(2,1)S(1)} %fusion.18), channel_id=1, replica_groups=mesh['hid'=8,'wid'=4] {'hid'}, dimensions={0}, use_global_device_ids=true | all-gather | bytes 294912 | tf_op jit(solution)/shard_map/all_gather | solution.py:17
  155.3 0.1 reshape.3
  155.4 11.2 %fusion.3 = bf16[32,1,3328]{2,0,1:T(8,128)(2,1)S(1)} fusion(bf16[32,4096]{1,0:T(8,128)(2,1)S(1)} %reshape.3, bf16[4096,3328]{1,0:T(8,128)(2,1)} %param.6), kind=kOutput, calls=%fused_computation.7 | convolution fusion | flops 872521728 | bytes 27738112 | tf_op jit(solution)/shard_map/dot_general | solution.py:19
  166.6 11.2 %fusion.2 = bf16[32,1,3328]{2,0,1:T(8,128)(2,1)S(1)} fusion(bf16[32,4096]{1,0:T(8,128)(2,1)S(1)} %reshape.3, bf16[4096,3328]{1,0:T(8,128)(2,1)} %param.5), kind=kOutput, calls=%fused_computation.6 | convolution fusion | flops 872521728 | bytes 27738112 | tf_op jit(solution)/shard_map/dot_general | solution.py:18
  177.8 0.8 pad_maximum_fusion.1
  178.6 0.0 all-reduce.9.cloned.1.call-update
  178.6 0.0 all-reduce.13.cloned.1.call-start
  178.7 37.3 %all-reduce.9.cloned.1.call-done = bf16[32,2,3328]{2,0,1:T(8,128)(2,1)} async-done(((bf16[32,2,3328]{2,0,1:T(8,128)(2,1)}), bf16[32,2,3328]{2,0,1:T(8,128)(2,1)}) %all-reduce.9.cloned.1.call-update) | async-done | bytes 426000 | tf_op jit(solution)/shard_map/psum | solution.py:10
  216.0 1.1 convert_element_type.31
  217.0 12.0 %fusion.10 = f32[32,4096]{1,0:T(8,128)} fusion(bf16[3328,4096]{1,0:T(8,128)(2,1)} %param.7, f32[32,2,3328]{2,0,1:T(8,128)S(1)} %convert_element_type.31), kind=kOutput, calls=%fused_computation.19 | convolution fusion | flops 873054208 | bytes 28639232 | tf_op jit(solution)/shard_map/dot_general | solution.py:23
  229.1 0.0 all-reduce.13.cloned.1.call-update
  229.1 54.2 %all-reduce.13.cloned.1.call-done = f32[32,4096]{1,0:T(8,128)} async-done(((f32[32,4096]{1,0:T(8,128)}), f32[32,4096]{1,0:T(8,128)}) %all-reduce.13.cloned.1.call-update) | async-done | bytes 524304
  283.2 1.6 fusion.14
Async XLA Ops:
  6.5 72.0 %all-reduce.7.cloned.1.call-start = ((), (), s32[]{:S(2)}) async-start(), calls=%async_computation | async-start | bytes 851968 | tf_op jit(solution)/shard_map/psum | solution.py:10
  40.0 51.7 %copy-start.1 = (u32[32]{0:T(128)S(1)}, u32[32]{0:T(128)}, u32[]{:S(2)}) copy-start(u32[32]{0:T(128)} %constant.7) | copy-start | bytes 388
  40.0 105.8 %copy-start = (bf16[4,4096]{1,0:T(4,128)(2,1)S(1)}, bf16[4,4096]{1,0:T(4,128)(2,1)}, u32[]{:S(2)}) copy-start(bf16[4,4096]{1,0:T(4,128)(2,1)} %param.4) | copy-start | bytes 98308
  40.9 104.9 %all-reduce.11.cloned.1.call-start = ((), (), s32[]{:S(2)}) async-start(), calls=%async_computation.2 | async-start | bytes 1048576
  91.6 124.3 %all-reduce.9.cloned.1.call-start = ((), (), s32[]{:S(2)}) async-start(), calls=%async_computation.1 | async-start | bytes 851968 | tf_op jit(solution)/shard_map/psum | solution.py:10
  178.6 104.6 %all-reduce.13.cloned.1.call-start = ((), (), s32[]{:S(2)}) async-start(), calls=%async_computation.3 | async-start | bytes 1048576
Sparse Core Ops, SparseCore 0:
  41.0 37.5 all-reduce.6
  91.8 53.9 all-reduce.10
  178.7 37.1 all-reduce.8
  229.2 53.9 all-reduce.12
where the time goes:
time: 292 us; the launch traced here: 291 us
  waiting for transfers between devices  182 us (62%)
  matrix products  68.9 us (24%)
  blocking collectives  19.5 us (7%)
  between operations  13.9 us (5%)
  other arithmetic  6.29 us (2%)
    unnamed x6, waiting for transfers between devices  107 us
    psum x2, waiting for transfers between devices, activate(): lax.psum(partial_value.astype(jnp.bfloat16), 'wid').astype(jnp.float32)  74.9 us
    dot_general x2, matrix products, per_device(): jnp.dot(hidden, down_weight, preferred_element_type=jnp.float32)  24.1 us
    dot_general x2, matrix products, per_device(): up_part = jnp.dot(shard_rows, up_weight, preferred_element_type=jnp.float32)  22.4 us
    dot_general x2, matrix products, per_device(): jnp.dot(shard_rows, gate_weight, preferred_element_type=jnp.float32)  22.4 us
    all_gather x2, blocking collectives, per_device(): shard_rows = lax.all_gather(stream, 'hid', axis=0, tiled=True)  19.5 us
  transfers between devices with their start and end apart: 4, of which 4 were waited for; matrix products, arithmetic and copies ran while one was open for 0% of the time, Pallas kernels for 0%

commit v1 on v0

--- a/solution.py
+++ b/solution.py
@@ -1,9 +1,20 @@
+import functools
+
 import jax
 import jax.numpy as jnp
 from jax import lax
+from jax.experimental import pallas as pl
+from jax.experimental.pallas import tpu as pltpu
 from jax.sharding import PartitionSpec as P
 
 STEPS = 2
+MESH = pl.DeviceIdType.MESH
+LANES = 128
+TALL = 16
+UNITS = 256
+KEEP = 5
+RING = 9
+LAG = 4
 
 
 def activate(partial_value):
@@ -11,7 +22,7 @@
     return (jax.nn.silu(totals[:, 0]) * totals[:, 1]).astype(jnp.bfloat16)
 
 
-def per_device(tokens, gate_weight, up_weight, down_weight):
+def plain(tokens, gate_weight, up_weight, down_weight):
     stream = tokens
     for repeat in range(STEPS):
         shard_rows = lax.all_gather(stream, "hid", axis=0, tiled=True)
@@ -29,9 +40,308 @@
     return stream
 
 
+def landed(ref, sem):
+    pltpu.make_async_copy(ref, ref, sem).wait()
+
+
+def kernel(
+    n_hid, n_wid, keep, ring, lag,
+    tok_ref, gate_ref, up_ref, down_ref, out_ref,
+    slots, x_wide, x_all, x_got, own, product, p_send, p_got, h_got, h_all,
+    branch, d_send, d_got, d_own, out_wide,
+    slot_sem, x_sems, p_send_sem, p_sem, h_sems, d_sems,
+):
+    f32, bf16 = jnp.float32, jnp.bfloat16
+    hid, wid = lax.axis_index("hid"), lax.axis_index("wid")
+    rows, width = tok_ref.shape
+    hidden = gate_ref.shape[1]
+    fold = TALL // rows
+    cols = fold * LANES
+    n_up, n_down = hidden // UNITS, width // cols
+    group = TALL // 2
+    streamed = n_up - keep + n_down
+
+    def fetch_up(j, slot):
+        off = pl.ds(pl.multiple_of(j * UNITS, UNITS), UNITS)
+        return [
+            pltpu.make_async_copy(
+                ref.at[:, off],
+                slots.at[slot, pl.ds(0, width), pl.ds(half * UNITS, UNITS)],
+                slot_sem.at[slot, half],
+            )
+            for half, ref in enumerate((gate_ref, up_ref))
+        ]
+
+    def fetch_down(c, slot):
+        off = pl.ds(pl.multiple_of(c * cols, cols), cols)
+        return pltpu.make_async_copy(
+            down_ref.at[:, off], slots.at[slot, pl.ds(0, hidden), :], slot_sem.at[slot, 0]
+        )
+
+    def start(q):
+        slot = keep + q % ring
+        k = q % streamed + keep
+
+        @pl.when(jnp.logical_and(q < STEPS * streamed, k < n_up))
+        def _():
+            for copy in fetch_up(k, slot):
+                copy.start()
+
+        @pl.when(jnp.logical_and(q < STEPS * streamed, k >= n_up))
+        def _():
+            fetch_down(k - n_up, slot).start()
+
+    @pl.loop(0, keep)
+    def _(j):
+        for copy in fetch_up(j, j):
+            copy.start()
+
+    @pl.loop(0, ring)
+    def _(q):
+        start(q)
+
+    barrier = pltpu.get_barrier_semaphore()
+
+    for d in range(1, n_hid):
+        pl.semaphore_signal(
+            barrier, inc=1, device_id=((hid + d) % n_hid, wid), device_id_type=MESH
+        )
+    for d in range(1, n_wid):
+        pl.semaphore_signal(
+            barrier, inc=1, device_id=(hid, (wid + d) % n_wid), device_id_type=MESH
+        )
+
+    for c in range(n_down):
+        for f in range(fold):
+            off = c * cols + f * LANES
+            own[c, f * rows:(f + 1) * rows, :] = tok_ref[:, off:off + LANES].astype(f32)
+
+    pl.semaphore_wait(barrier, n_hid + n_wid - 2)
+
+    def step(s, carry):
+        x_got[s, hid] = own[...].astype(bf16)
+        for d in range(1, n_hid):
+            pltpu.make_async_remote_copy(
+                src_ref=x_got.at[s, hid],
+                dst_ref=x_got.at[s, hid],
+                send_sem=x_sems.at[s, 0],
+                recv_sem=x_sems.at[s, 1],
+                device_id=((hid + d) % n_hid, wid),
+                device_id_type=MESH,
+            ).start()
+        landed(x_got.at[s, pl.ds(0, n_hid - 1)], x_sems.at[s, 1])
+        for h in range(n_hid):
+            for c in range(n_down):
+                block = x_got[s, h, c].astype(f32)
+                for f in range(fold):
+                    off = c * cols + f * LANES
+                    x_wide[h * rows:(h + 1) * rows, off:off + LANES] = block[
+                        f * rows:(f + 1) * rows, :
+                    ]
+        x_all[...] = x_wide[...].astype(bf16)
+
+        def finish(j):
+            landed(p_got.at[s, j], p_sem.at[s, j])
+            total = p_send[s, j, wid].astype(f32)
+            for d in range(n_wid - 1):
+                total = total + p_got[s, j, d].astype(f32)
+            gate, up = total[:group, :], total[group:, :]
+            value = gate / (1.0 + jnp.exp(-gate)) * up
+            h_got[s, j, wid] = jnp.concatenate(
+                [value[:, :LANES], value[:, LANES:]], axis=0
+            ).astype(bf16)
+            for d in range(1, n_wid):
+                pltpu.make_async_remote_copy(
+                    src_ref=h_got.at[s, j, wid],
+                    dst_ref=h_got.at[s, j, wid],
+                    send_sem=h_sems.at[s, 0],
+                    recv_sem=h_sems.at[s, 1],
+                    device_id=(hid, (wid + d) % n_wid),
+                    device_id_type=MESH,
+                ).start()
+
+        @pl.loop(0, n_up)
+        def _(j):
+            q = s * streamed + j - keep
+            kept = j < keep
+            slot = jnp.where(kept, j, keep + (q + ring) % ring)
+
+            @pl.when(jnp.logical_or(s == 0, jnp.logical_not(kept)))
+            def _():
+                for copy in fetch_up(j, slot):
+                    copy.wait()
+
+            product[...] = jnp.dot(
+                x_all[...], slots[slot, :width, :], preferred_element_type=f32
+            )
+            for w in range(n_wid):
+                lo = w * group
+                p_send[s, j, w] = jnp.concatenate(
+                    [product[lo:lo + group, :UNITS], product[lo:lo + group, UNITS:]], axis=0
+                ).astype(bf16)
+            for d in range(1, n_wid):
+                peer = (wid + d) % n_wid
+                pltpu.make_async_remote_copy(
+                    src_ref=p_send.at[s, j, peer],
+                    dst_ref=p_got.at[s, j, d - 1],
+                    send_sem=p_send_sem.at[s],
+                    recv_sem=p_sem.at[s, j],
+                    device_id=(hid, peer),
+                    device_id_type=MESH,
+                ).start()
+
+            @pl.when(jnp.logical_not(kept))
+            def _():
+                start(q + ring)
+
+            @pl.when(j >= lag)
+            def _():
+                finish(j - lag)
+
+        @pl.loop(n_up - lag, n_up)
+        def _(j):
+            finish(j)
+
+        landed(h_got.at[s, :, pl.ds(0, n_wid - 1)], h_sems.at[s, 1])
+        for j in range(n_up):
+            block = h_got[s, j].astype(f32)
+            for half in range(2):
+                off = j * UNITS + half * LANES
+                h_all[:, off:off + LANES] = (
+                    block[:, half * group:(half + 1) * group, :]
+                    .reshape(n_wid * group, LANES)
+                    .astype(bf16)
+                )
+
+        @pl.loop(0, n_down)
+        def _(c):
+            q = s * streamed + n_up - keep + c
+            slot = keep + q % ring
+            fetch_down(c, slot).wait()
+            x_wide[:, :cols] = jnp.dot(
+                h_all[...], slots[slot, :hidden, :], preferred_element_type=f32
+            )
+            for h in range(n_hid):
+                for f in range(fold):
+                    branch[h, f * rows:(f + 1) * rows, :] = x_wide[
+                        h * rows:(h + 1) * rows, f * LANES:(f + 1) * LANES
+                    ]
+            d_send[s, c] = branch[...].astype(bf16)
+            d_own[c] = branch[hid]
+            for d in range(1, n_hid):
+                peer = (hid + d) % n_hid
+                pltpu.make_async_remote_copy(
+                    src_ref=d_send.at[s, c, peer],
+                    dst_ref=d_got.at[s, c, d - 1],
+                    send_sem=d_sems.at[s, 0],
+                    recv_sem=d_sems.at[s, 1],
+                    device_id=(peer, wid),
+                    device_id_type=MESH,
+                ).start()
+            start(q + ring)
+
+        landed(d_got.at[s], d_sems.at[s, 1])
+        total = d_own[...]
+        for d in range(n_hid - 1):
+            total = total + d_got[s, :, d].astype(f32)
+        own[...] = (own[...] + total).astype(bf16).astype(f32)
+
+        landed(x_got.at[s, pl.ds(0, n_hid - 1)], x_sems.at[s, 0])
+        landed(p_send.at[s, :, pl.ds(0, n_wid - 1)], p_send_sem.at[s])
+        landed(h_got.at[s, :, pl.ds(0, n_wid - 1)], h_sems.at[s, 0])
+        landed(d_send.at[s, :, pl.ds(0, n_hid - 1)], d_sems.at[s, 0])
+        return carry
+
+    lax.fori_loop(0, STEPS, step, 0)
+
+    for c in range(n_down):
+        for f in range(fold):
+            off = c * cols + f * LANES
+            out_wide[:, off:off + LANES] = own[c, f * rows:(f + 1) * rows, :]
+    out_ref[...] = out_wide[...].astype(bf16)
+
+
+def fused(n_hid, n_wid, tokens, gate_weight, up_weight, down_weight):
+    rows, width = tokens.shape
+    hidden = gate_weight.shape[1]
+    fold = TALL // rows
+    cols = fold * LANES
+    n_up, n_down = hidden // UNITS, width // cols
+    keep = min(KEEP, n_up - 1)
+    ring = min(RING, n_up - keep + n_down)
+    lag = min(LAG, n_up - 1)
+    all_rows = n_hid * rows
+    bf16, f32 = jnp.bfloat16, jnp.float32
+    dma = pltpu.SemaphoreType.DMA
+    weights = 3 * width * hidden
+    return pl.pallas_call(
+        functools.partial(kernel, n_hid, n_wid, keep, ring, lag),
+        out_shape=jax.ShapeDtypeStruct((rows, width), bf16),
+        in_specs=[pl.BlockSpec(memory_space=pltpu.VMEM)]
+        + [pl.BlockSpec(memory_space=pl.ANY)] * 3,
+        out_specs=pl.BlockSpec(memory_space=pltpu.VMEM),
+        scratch_shapes=[
+            pltpu.VMEM((keep + ring, max(width, hidden), 2 * UNITS), bf16),
+            pltpu.VMEM((all_rows, width), f32),
+            pltpu.VMEM((all_rows, width), bf16),
+            pltpu.VMEM((STEPS, n_hid, n_down, TALL, LANES), bf16),
+            pltpu.VMEM((n_down, TALL, LANES), f32),
+            pltpu.VMEM((all_rows, 2 * UNITS), f32),
+            pltpu.VMEM((STEPS, n_up, n_wid, TALL, UNITS), bf16),
+            pltpu.VMEM((STEPS, n_up, n_wid - 1, TALL, UNITS), bf16),
+            pltpu.VMEM((STEPS, n_up, n_wid, TALL, LANES), bf16),
+            pltpu.VMEM((all_rows, hidden), bf16),
+            pltpu.VMEM((n_hid, TALL, LANES), f32),
+            pltpu.VMEM((STEPS, n_down, n_hid, TALL, LANES), bf16),
+            pltpu.VMEM((STEPS, n_down, n_hid - 1, TALL, LANES), bf16),
+            pltpu.VMEM((n_down, TALL, LANES), f32),
+            pltpu.VMEM((rows, width), f32),
+            dma((keep + ring, 2)),
+            dma((STEPS, 2)),
+            dma((STEPS,)),
+            dma((STEPS, n_up)),
+            dma((STEPS, 2)),
+            dma((STEPS, 2)),
+        ],
+        compiler_params=pltpu.CompilerParams(
+            collective_id=0, has_side_effects=True, vmem_limit_bytes=VMEM_BYTES
+        ),
+        cost_estimate=pl.CostEstimate(
+            flops=STEPS * 2 * all_rows * weights,
+            bytes_accessed=STEPS * 2 * weights,
+            transcendentals=STEPS * all_rows * hidden,
+        ),
+    )(tokens, gate_weight, up_weight, down_weight)
+
+
+VMEM_BYTES = 64 * 1024 * 1024 - 64 * 1024
+
+
+def per_device(n_hid, n_wid, tokens, gate_weight, up_weight, down_weight):
+    rows, width = tokens.shape
+    hidden = gate_weight.shape[1]
+    fits = (
+        TALL % rows == 0
+        and n_hid > 1
+        and n_wid > 1
+        and n_hid * rows == n_wid * (TALL // 2)
+        and hidden % UNITS == 0
+        and hidden >= 2 * UNITS
+        and (TALL // rows) * LANES == 2 * UNITS
+        and width % (2 * UNITS) == 0
+    )
+    if fits:
+        return fused(n_hid, n_wid, tokens, gate_weight, up_weight, down_weight)
+    return plain(tokens, gate_weight, up_weight, down_weight)
+
+
 def solution(mesh):
     in_specs = (P("hid", "wid"), P("wid", "hid"), P("wid", "hid"), P("hid", "wid"))
     out_specs = P("hid", "wid")
     return jax.shard_map(
-        per_device, mesh=mesh, in_specs=in_specs, out_specs=out_specs, check_vma=False
+        functools.partial(per_device, mesh.shape["hid"], mesh.shape["wid"]),
+        mesh=mesh,
+        in_specs=in_specs,
+        out_specs=out_specs,
+        check_vma=False,
     )

time: 292 us -> 77.2 us (0.26)
  waiting for transfers between devices: 182 us -> 0 us
  Pallas kernels: 0 us -> 75.5 us
  matrix products: 68.9 us -> 0 us
  blocking collectives: 19.5 us -> 0 us
  between operations: 13.9 us -> 0.01 us
  other arithmetic: 6.29 us -> 0 us
    unnamed x6 -> x0, waiting for transfers between devices: 107 us -> none
    pallas_call x0 -> x1, Pallas kernels: none -> 75.5 us  [fused(): pl.pallas_call(functools.partial(kernel, n_hid, n_wid, keep, ring, lag),...]
    psum x2 -> x0, waiting for transfers between devices: 74.9 us -> none  [activate(): lax.psum(partial_value.astype(jnp.bfloat16), 'wid').astype(jnp.float32)]
    dot_general x6 -> x0, matrix products: 68.9 us -> none  [the longest x2 24.1 us: per_device(): jnp.dot(hidden, down_weight, preferred_element_type=jnp.float32)]
    all_gather x2 -> x0, blocking collectives: 19.5 us -> none  [per_device(): shard_rows = lax.all_gather(stream, 'hid', axis=0, tiled=True)]
    convert_element_type x3 -> x0, other arithmetic: 3.75 us -> none  [the longest x2 2.13 us: activate(): lax.psum(partial_value.astype(jnp.bfloat16), 'wid').astype(jnp.float32)]
  transfers between devices with their start and end apart: 4 -> 0, of which waited for: 4 -> 0; matrix products, arithmetic and copies ran while one was open for 0% -> 0% of each run, Pallas kernels for 0% -> 0%
where the time goes in v1:
time: 77.2 us; the launch traced here: 76.9 us
  Pallas kernels  75.5 us (98%)
  local copies, waits for them, and re-layouts  1.39 us (2%)
    pallas_call x1, Pallas kernels, fused(): pl.pallas_call(functools.partial(kernel, n_hid, n_wid, keep, ring, lag),...  75.5 us

profile of v1, /device:TPU:0, one launch (start us, length us, event | category | flops | bytes accessed | tf_op | source)
XLA Modules:
  0.0 76.9 jit_solution(1379408081999540442)
XLA Ops:
  0.0 75.5 %shard_map.46 = bf16[4,4096]{1,0:T(4,128)(2,1)} custom-call(bf16[4,4096]{1,0:T(4,128)(2,1)} %tok_ref.1, bf16[4096,3328]{1,0:T(8,128)(2,1)} %gate_ref.1, bf16[4096,3328]{1,0:T(8,128)(2,1)} %up_ref.1, bf16[3328,4096]{1,0:T(8,128)(2,1)} %down_ref.1), custom_call_target="tpu_custom_call" | custom-call | flops 5234491392 | bytes 163577856 | tf_op jit(solution)/shard_map/pallas_call | solution.py:277
  75.5 1.4 %copy.6 = bf16[4,4096]{1,0:T(4,128)(2,1)} copy(bf16[4,4096]{1,0:T(4,128)(2,1)} %shard_map.46) | data formatting | bytes 65536

commit v2 on v1

--- a/solution.py
+++ b/solution.py
@@ -14,7 +14,7 @@
 UNITS = 256
 KEEP = 5
 RING = 9
-LAG = 4
+LAG = 3
 
 
 def activate(partial_value):
@@ -45,10 +45,10 @@
 
 
 def kernel(
-    n_hid, n_wid, keep, ring, lag,
+    n_hid, n_wid, keep, ring, lag, early,
     tok_ref, gate_ref, up_ref, down_ref, out_ref,
     slots, x_wide, x_all, x_got, own, product, p_send, p_got, h_got, h_all,
-    branch, d_send, d_got, d_own, out_wide,
+    partial, branch, d_send, d_got, d_own, out_wide,
     slot_sem, x_sems, p_send_sem, p_sem, h_sems, d_sems,
 ):
     f32, bf16 = jnp.float32, jnp.bfloat16
@@ -59,7 +59,9 @@
     cols = fold * LANES
     n_up, n_down = hidden // UNITS, width // cols
     group = TALL // 2
-    streamed = n_up - keep + n_down
+    n_pair = n_down // 2
+    streamed = n_up - keep + 2 * n_pair
+    k_early, k_late = early * UNITS, hidden - early * UNITS
 
     def fetch_up(j, slot):
         off = pl.ds(pl.multiple_of(j * UNITS, UNITS), UNITS)
@@ -72,11 +74,19 @@
             for half, ref in enumerate((gate_ref, up_ref))
         ]
 
-    def fetch_down(c, slot):
-        off = pl.ds(pl.multiple_of(c * cols, cols), cols)
-        return pltpu.make_async_copy(
-            down_ref.at[:, off], slots.at[slot, pl.ds(0, hidden), :], slot_sem.at[slot, 0]
-        )
+    def fetch_down(c, slot, late):
+        top, depth = (k_early, k_late) if late else (0, k_early)
+        return [
+            pltpu.make_async_copy(
+                down_ref.at[
+                    pl.ds(top, depth),
+                    pl.ds(pl.multiple_of((2 * c + half) * cols, cols), cols),
+                ],
+                slots.at[slot, pl.ds(half * depth, depth), :],
+                slot_sem.at[slot, half],
+            )
+            for half in range(2)
+        ]
 
     def start(q):
         slot = keep + q % ring
@@ -87,9 +97,17 @@
             for copy in fetch_up(k, slot):
                 copy.start()
 
-        @pl.when(jnp.logical_and(q < STEPS * streamed, k >= n_up))
+        in_early = jnp.logical_and(k >= n_up, k < n_up + n_pair)
+
+        @pl.when(jnp.logical_and(q < STEPS * streamed, in_early))
         def _():
-            fetch_down(k - n_up, slot).start()
+            for copy in fetch_down(k - n_up, slot, False):
+                copy.start()
+
+        @pl.when(jnp.logical_and(q < STEPS * streamed, k >= n_up + n_pair))
+        def _():
+            for copy in fetch_down(k - n_up - n_pair, slot, True):
+                copy.start()
 
     @pl.loop(0, keep)
     def _(j):
@@ -141,7 +159,6 @@
         x_all[...] = x_wide[...].astype(bf16)
 
         def finish(j):
-            landed(p_got.at[s, j], p_sem.at[s, j])
             total = p_send[s, j, wid].astype(f32)
             for d in range(n_wid - 1):
                 total = total + p_got[s, j, d].astype(f32)
@@ -150,18 +167,20 @@
             h_got[s, j, wid] = jnp.concatenate(
                 [value[:, :LANES], value[:, LANES:]], axis=0
             ).astype(bf16)
+
+        def share(j):
+            late = jnp.where(j >= early, 1, 0)
             for d in range(1, n_wid):
                 pltpu.make_async_remote_copy(
                     src_ref=h_got.at[s, j, wid],
                     dst_ref=h_got.at[s, j, wid],
-                    send_sem=h_sems.at[s, 0],
-                    recv_sem=h_sems.at[s, 1],
+                    send_sem=h_sems.at[s, 2],
+                    recv_sem=h_sems.at[s, late],
                     device_id=(hid, (wid + d) % n_wid),
                     device_id_type=MESH,
                 ).start()
 
-        @pl.loop(0, n_up)
-        def _(j):
+        def piece(j, with_finish):
             q = s * streamed + j - keep
             kept = j < keep
             slot = jnp.where(kept, j, keep + (q + ring) % ring)
@@ -171,6 +190,9 @@
                 for copy in fetch_up(j, slot):
                     copy.wait()
 
+            if with_finish:
+                landed(p_got.at[s, j - lag], p_sem.at[s, j - lag])
+                finish(j - lag)
             product[...] = jnp.dot(
                 x_all[...], slots[slot, :width, :], preferred_element_type=f32
             )
@@ -189,55 +211,107 @@
                     device_id=(hid, peer),
                     device_id_type=MESH,
                 ).start()
+            if with_finish:
+                share(j - lag)
 
             @pl.when(jnp.logical_not(kept))
             def _():
                 start(q + ring)
 
-            @pl.when(j >= lag)
-            def _():
-                finish(j - lag)
-
-        @pl.loop(n_up - lag, n_up)
+        @pl.loop(0, lag)
         def _(j):
-            finish(j)
-
-        landed(h_got.at[s, :, pl.ds(0, n_wid - 1)], h_sems.at[s, 1])
-        for j in range(n_up):
-            block = h_got[s, j].astype(f32)
-            for half in range(2):
-                off = j * UNITS + half * LANES
-                h_all[:, off:off + LANES] = (
-                    block[:, half * group:(half + 1) * group, :]
-                    .reshape(n_wid * group, LANES)
-                    .astype(bf16)
-                )
-
-        @pl.loop(0, n_down)
-        def _(c):
+            piece(j, False)
+
+        @pl.loop(lag, n_up)
+        def _(j):
+            piece(j, True)
+
+        def gather_hidden(first, last, sem):
+            landed(
+                h_got.at[s, pl.ds(first, last - first), pl.ds(0, n_wid - 1)],
+                h_sems.at[s, sem],
+            )
+            for j in range(first, last):
+                block = h_got[s, j].astype(f32)
+                for half in range(2):
+                    off = j * UNITS + half * LANES
+                    h_all[:, off:off + LANES] = (
+                        block[:, half * group:(half + 1) * group, :]
+                        .reshape(n_wid * group, LANES)
+                        .astype(bf16)
+                    )
+
+        gather_hidden(0, early, 0)
+
+        def early_pair(c, with_finish):
             q = s * streamed + n_up - keep + c
             slot = keep + q % ring
-            fetch_down(c, slot).wait()
-            x_wide[:, :cols] = jnp.dot(
-                h_all[...], slots[slot, :hidden, :], preferred_element_type=f32
-            )
-            for h in range(n_hid):
-                for f in range(fold):
-                    branch[h, f * rows:(f + 1) * rows, :] = x_wide[
-                        h * rows:(h + 1) * rows, f * LANES:(f + 1) * LANES
-                    ]
-            d_send[s, c] = branch[...].astype(bf16)
-            d_own[c] = branch[hid]
-            for d in range(1, n_hid):
-                peer = (hid + d) % n_hid
-                pltpu.make_async_remote_copy(
-                    src_ref=d_send.at[s, c, peer],
-                    dst_ref=d_got.at[s, c, d - 1],
-                    send_sem=d_sems.at[s, 0],
-                    recv_sem=d_sems.at[s, 1],
-                    device_id=(peer, wid),
-                    device_id_type=MESH,
-                ).start()
+            for copy in fetch_down(c, slot, False):
+                copy.wait()
+            if with_finish:
+                j = n_up - lag + c
+                landed(p_got.at[s, j], p_sem.at[s, j])
+                finish(j)
+            for half in range(2):
+                lo = half * k_early
+                partial[2 * c + half] = jnp.dot(
+                    h_all[:, :k_early],
+                    slots[slot, lo:lo + k_early, :],
+                    preferred_element_type=f32,
+                )
+            if with_finish:
+                share(j)
+            start(q + ring)
+
+        both = min(lag, n_pair)
+
+        @pl.loop(0, both)
+        def _(c):
+            early_pair(c, True)
+
+        @pl.loop(both, n_pair)
+        def _(c):
+            early_pair(c, False)
+
+        @pl.loop(n_up - lag + both, n_up)
+        def _(j):
+            landed(p_got.at[s, j], p_sem.at[s, j])
+            finish(j)
+            share(j)
+
+        gather_hidden(early, n_up, 1)
+
+        @pl.loop(0, n_pair)
+        def _(pair):
+            q = s * streamed + n_up - keep + n_pair + pair
+            slot = keep + q % ring
+            for copy in fetch_down(pair, slot, True):
+                copy.wait()
+            for half in range(2):
+                c = 2 * pair + half
+                lo = half * k_late
+                x_wide[:, :cols] = partial[c] + jnp.dot(
+                    h_all[:, k_early:],
+                    slots[slot, lo:lo + k_late, :],
+                    preferred_element_type=f32,
+                )
+                for h in range(n_hid):
+                    for f in range(fold):
+                        branch[h, f * rows:(f + 1) * rows, :] = x_wide[
+                            h * rows:(h + 1) * rows, f * LANES:(f + 1) * LANES
+                        ]
+                d_send[s, c] = branch[...].astype(bf16)
+                d_own[c] = branch[hid]
+                for d in range(1, n_hid):
+                    peer = (hid + d) % n_hid
+                    pltpu.make_async_remote_copy(
+                        src_ref=d_send.at[s, c, peer],
+                        dst_ref=d_got.at[s, c, d - 1],
+                        send_sem=d_sems.at[s, 0],
+                        recv_sem=d_sems.at[s, 1],
+                        device_id=(peer, wid),
+                        device_id_type=MESH,
+                    ).start()
             start(q + ring)
 
         landed(d_got.at[s], d_sems.at[s, 1])
@@ -248,7 +322,7 @@
 
         landed(x_got.at[s, pl.ds(0, n_hid - 1)], x_sems.at[s, 0])
         landed(p_send.at[s, :, pl.ds(0, n_wid - 1)], p_send_sem.at[s])
-        landed(h_got.at[s, :, pl.ds(0, n_wid - 1)], h_sems.at[s, 0])
+        landed(h_got.at[s, :, pl.ds(0, n_wid - 1)], h_sems.at[s, 2])
         landed(d_send.at[s, :, pl.ds(0, n_hid - 1)], d_sems.at[s, 0])
         return carry
 
@@ -270,18 +344,20 @@
     keep = min(KEEP, n_up - 1)
     ring = min(RING, n_up - keep + n_down)
     lag = min(LAG, n_up - 1)
+    early = max(1, n_up * 5 // 8)
+    slot_rows = max(width, 2 * UNITS * max(early, n_up - early))
     all_rows = n_hid * rows
     bf16, f32 = jnp.bfloat16, jnp.float32
     dma = pltpu.SemaphoreType.DMA
     weights = 3 * width * hidden
     return pl.pallas_call(
-        functools.partial(kernel, n_hid, n_wid, keep, ring, lag),
+        functools.partial(kernel, n_hid, n_wid, keep, ring, lag, early),
         out_shape=jax.ShapeDtypeStruct((rows, width), bf16),
         in_specs=[pl.BlockSpec(memory_space=pltpu.VMEM)]
         + [pl.BlockSpec(memory_space=pl.ANY)] * 3,
         out_specs=pl.BlockSpec(memory_space=pltpu.VMEM),
         scratch_shapes=[
-            pltpu.VMEM((keep + ring, max(width, hidden), 2 * UNITS), bf16),
+            pltpu.VMEM((keep + ring, slot_rows, 2 * UNITS), bf16),
             pltpu.VMEM((all_rows, width), f32),
             pltpu.VMEM((all_rows, width), bf16),
             pltpu.VMEM((STEPS, n_hid, n_down, TALL, LANES), bf16),
@@ -291,6 +367,7 @@
             pltpu.VMEM((STEPS, n_up, n_wid - 1, TALL, UNITS), bf16),
             pltpu.VMEM((STEPS, n_up, n_wid, TALL, LANES), bf16),
             pltpu.VMEM((all_rows, hidden), bf16),
+            pltpu.VMEM((n_down, all_rows, cols), f32),
             pltpu.VMEM((n_hid, TALL, LANES), f32),
             pltpu.VMEM((STEPS, n_down, n_hid, TALL, LANES), bf16),
             pltpu.VMEM((STEPS, n_down, n_hid - 1, TALL, LANES), bf16),
@@ -300,7 +377,7 @@
             dma((STEPS, 2)),
             dma((STEPS,)),
             dma((STEPS, n_up)),
-            dma((STEPS, 2)),
+            dma((STEPS, 3)),
             dma((STEPS, 2)),
         ],
         compiler_params=pltpu.CompilerParams(
@@ -328,7 +405,7 @@
         and hidden % UNITS == 0
         and hidden >= 2 * UNITS
         and (TALL // rows) * LANES == 2 * UNITS
-        and width % (2 * UNITS) == 0
+        and width % (4 * UNITS) == 0
     )
     if fits:
         return fused(n_hid, n_wid, tokens, gate_weight, up_weight, down_weight)

time: 77.2 us -> 85 us (1.10)
  Pallas kernels: 75.5 us -> 83.4 us
    pallas_call x1, Pallas kernels: 75.5 us -> 83.4 us  [fused(): pl.pallas_call(functools.partial(kernel, n_hid, n_wid, keep, ring, lag, e...]
where the time goes in v2:
time: 85 us; the launch traced here: 84.8 us
  Pallas kernels  83.4 us (98%)
  local copies, waits for them, and re-layouts  1.39 us (2%)
    pallas_call x1, Pallas kernels, fused(): pl.pallas_call(functools.partial(kernel, n_hid, n_wid, keep, ring, lag, e...  83.4 us

profile of v2, /device:TPU:0, one launch (start us, length us, event | category | flops | bytes accessed | tf_op | source)
XLA Modules:
  0.0 84.8 jit_solution(7887316258927789478)
XLA Ops:
  0.0 83.4 %shard_map.46 = bf16[4,4096]{1,0:T(4,128)(2,1)} custom-call(bf16[4,4096]{1,0:T(4,128)(2,1)} %tok_ref.1, bf16[4096,3328]{1,0:T(8,128)(2,1)} %gate_ref.1, bf16[4096,3328]{1,0:T(8,128)(2,1)} %up_ref.1, bf16[3328,4096]{1,0:T(8,128)(2,1)} %down_ref.1), custom_call_target="tpu_custom_call" | custom-call | flops 5234491392 | bytes 163577856 | tf_op jit(solution)/shard_map/pallas_call | solution.py:353
  83.4 1.4 %copy.6 = bf16[4,4096]{1,0:T(4,128)(2,1)} copy(bf16[4,4096]{1,0:T(4,128)(2,1)} %shard_map.46) | data formatting | bytes 65536

commit v3 on v1

--- a/solution.py
+++ b/solution.py
@@ -14,7 +14,7 @@
 UNITS = 256
 KEEP = 5
 RING = 9
-LAG = 4
+LAG = 5
 
 
 def activate(partial_value):
@@ -45,10 +45,10 @@
 
 
 def kernel(
-    n_hid, n_wid, keep, ring, lag,
+    n_hid, n_wid, keep, ring, lag, levels,
     tok_ref, gate_ref, up_ref, down_ref, out_ref,
     slots, x_wide, x_all, x_got, own, product, p_send, p_got, h_got, h_all,
-    branch, d_send, d_got, d_own, out_wide,
+    partial, branch, d_send, d_got, d_own, out_wide,
     slot_sem, x_sems, p_send_sem, p_sem, h_sems, d_sems,
 ):
     f32, bf16 = jnp.float32, jnp.bfloat16
@@ -59,7 +59,7 @@
     cols = fold * LANES
     n_up, n_down = hidden // UNITS, width // cols
     group = TALL // 2
-    streamed = n_up - keep + n_down
+    streamed = n_up - keep + levels[-1][3] + levels[-1][4]
 
     def fetch_up(j, slot):
         off = pl.ds(pl.multiple_of(j * UNITS, UNITS), UNITS)
@@ -72,11 +72,20 @@
             for half, ref in enumerate((gate_ref, up_ref))
         ]
 
-    def fetch_down(c, slot):
-        off = pl.ds(pl.multiple_of(c * cols, cols), cols)
-        return pltpu.make_async_copy(
-            down_ref.at[:, off], slots.at[slot, pl.ds(0, hidden), :], slot_sem.at[slot, 0]
-        )
+    def fetch_down(u, slot, level):
+        first, last, per = level[:3]
+        depth = (last - first) * UNITS
+        return [
+            pltpu.make_async_copy(
+                down_ref.at[
+                    pl.ds(first * UNITS, depth),
+                    pl.ds(pl.multiple_of((per * u + part) * cols, cols), cols),
+                ],
+                slots.at[slot, pl.ds(part * depth, depth), :],
+                slot_sem.at[slot, part],
+            )
+            for part in range(per)
+        ]
 
     def start(q):
         slot = keep + q % ring
@@ -87,9 +96,14 @@
             for copy in fetch_up(k, slot):
                 copy.start()
 
-        @pl.when(jnp.logical_and(q < STEPS * streamed, k >= n_up))
-        def _():
-            fetch_down(k - n_up, slot).start()
+        for level in levels:
+            u = k - n_up - level[4]
+            here = jnp.logical_and(u >= 0, u < level[3])
+
+            @pl.when(jnp.logical_and(q < STEPS * streamed, here))
+            def _():
+                for copy in fetch_down(u, slot, level):
+                    copy.start()
 
     @pl.loop(0, keep)
     def _(j):
@@ -141,7 +155,6 @@
         x_all[...] = x_wide[...].astype(bf16)
 
         def finish(j):
-            landed(p_got.at[s, j], p_sem.at[s, j])
             total = p_send[s, j, wid].astype(f32)
             for d in range(n_wid - 1):
                 total = total + p_got[s, j, d].astype(f32)
@@ -150,18 +163,20 @@
             h_got[s, j, wid] = jnp.concatenate(
                 [value[:, :LANES], value[:, LANES:]], axis=0
             ).astype(bf16)
+
+        def share(j):
+            level_of = sum(jnp.where(j >= level[0], 1, 0) for level in levels[1:])
             for d in range(1, n_wid):
                 pltpu.make_async_remote_copy(
                     src_ref=h_got.at[s, j, wid],
                     dst_ref=h_got.at[s, j, wid],
-                    send_sem=h_sems.at[s, 0],
-                    recv_sem=h_sems.at[s, 1],
+                    send_sem=h_sems.at[s, len(levels)],
+                    recv_sem=h_sems.at[s, level_of],
                     device_id=(hid, (wid + d) % n_wid),
                     device_id_type=MESH,
                 ).start()
 
-        @pl.loop(0, n_up)
-        def _(j):
+        def piece(j, with_finish):
             q = s * streamed + j - keep
             kept = j < keep
             slot = jnp.where(kept, j, keep + (q + ring) % ring)
@@ -171,6 +186,9 @@
                 for copy in fetch_up(j, slot):
                     copy.wait()
 
+            if with_finish:
+                landed(p_got.at[s, j - lag], p_sem.at[s, j - lag])
+                finish(j - lag)
             product[...] = jnp.dot(
                 x_all[...], slots[slot, :width, :], preferred_element_type=f32
             )
@@ -189,38 +207,44 @@
                     device_id=(hid, peer),
                     device_id_type=MESH,
                 ).start()
+            if with_finish:
+                share(j - lag)
 
             @pl.when(jnp.logical_not(kept))
             def _():
                 start(q + ring)
 
-            @pl.when(j >= lag)
-            def _():
-                finish(j - lag)
-
-        @pl.loop(n_up - lag, n_up)
+        @pl.loop(0, lag)
         def _(j):
-            finish(j)
-
-        landed(h_got.at[s, :, pl.ds(0, n_wid - 1)], h_sems.at[s, 1])
-        for j in range(n_up):
-            block = h_got[s, j].astype(f32)
-            for half in range(2):
-                off = j * UNITS + half * LANES
-                h_all[:, off:off + LANES] = (
-                    block[:, half * group:(half + 1) * group, :]
-                    .reshape(n_wid * group, LANES)
-                    .astype(bf16)
-                )
-
-        @pl.loop(0, n_down)
-        def _(c):
-            q = s * streamed + n_up - keep + c
-            slot = keep + q % ring
-            fetch_down(c, slot).wait()
-            x_wide[:, :cols] = jnp.dot(
-                h_all[...], slots[slot, :hidden, :], preferred_element_type=f32
+            piece(j, False)
+
+        @pl.loop(lag, n_up)
+        def _(j):
+            piece(j, True)
+
+        def gather_hidden(first, last, sem):
+            landed(
+                h_got.at[s, pl.ds(first, last - first), pl.ds(0, n_wid - 1)],
+                h_sems.at[s, sem],
             )
+            for j in range(first, last):
+                block = h_got[s, j].astype(f32)
+                for half in range(2):
+                    off = j * UNITS + half * LANES
+                    h_all[:, off:off + LANES] = (
+                        block[:, half * group:(half + 1) * group, :]
+                        .reshape(n_wid * group, LANES)
+                        .astype(bf16)
+                    )
+
+        def drain(first, last):
+            @pl.loop(first, last)
+            def _(j):
+                landed(p_got.at[s, j], p_sem.at[s, j])
+                finish(j)
+                share(j)
+
+        def spread(c):
             for h in range(n_hid):
                 for f in range(fold):
                     branch[h, f * rows:(f + 1) * rows, :] = x_wide[
@@ -238,7 +262,54 @@
                     device_id=(peer, wid),
                     device_id_type=MESH,
                 ).start()
+
+        def level_slot(u, index, finish_from):
+            level = levels[index]
+            first, last, per = level[:3]
+            depth = (last - first) * UNITS
+            q = s * streamed + n_up - keep + level[4] + u
+            slot = keep + q % ring
+            for copy in fetch_down(u, slot, level):
+                copy.wait()
+            if finish_from is not None:
+                j = finish_from + u
+                landed(p_got.at[s, j], p_sem.at[s, j])
+                finish(j)
+            for part in range(per):
+                c = per * u + part
+                term = jnp.dot(
+                    h_all[:, first * UNITS:last * UNITS],
+                    slots[slot, part * depth:(part + 1) * depth, :],
+                    preferred_element_type=f32,
+                )
+                if index == 0:
+                    partial[c] = term
+                elif index < len(levels) - 1:
+                    partial[c] = partial[c] + term
+                else:
+                    x_wide[:, :cols] = partial[c] + term
+                    spread(c)
+            if finish_from is not None:
+                share(j)
             start(q + ring)
+
+        done = n_up - lag
+        for index, level in enumerate(levels):
+            need = n_up if index == len(levels) - 1 else level[1]
+            if done < need:
+                drain(done, need)
+                done = need
+            gather_hidden(level[0], level[1], index)
+            more = 0 if index == len(levels) - 1 else min(level[3], n_up - done)
+            if more > 0:
+                pl.loop(0, more)(
+                    functools.partial(level_slot, index=index, finish_from=done)
+                )
+                done += more
+            if more < level[3]:
+                pl.loop(more, level[3])(
+                    functools.partial(level_slot, index=index, finish_from=None)
+                )
 
         landed(d_got.at[s], d_sems.at[s, 1])
         total = d_own[...]
@@ -248,7 +319,7 @@
 
         landed(x_got.at[s, pl.ds(0, n_hid - 1)], x_sems.at[s, 0])
         landed(p_send.at[s, :, pl.ds(0, n_wid - 1)], p_send_sem.at[s])
-        landed(h_got.at[s, :, pl.ds(0, n_wid - 1)], h_sems.at[s, 0])
+        landed(h_got.at[s, :, pl.ds(0, n_wid - 1)], h_sems.at[s, len(levels)])
         landed(d_send.at[s, :, pl.ds(0, n_hid - 1)], d_sems.at[s, 0])
         return carry
 
@@ -268,20 +339,29 @@
     cols = fold * LANES
     n_up, n_down = hidden // UNITS, width // cols
     keep = min(KEEP, n_up - 1)
-    ring = min(RING, n_up - keep + n_down)
-    lag = min(LAG, n_up - 1)
+    ring = RING
+    one = max(1, n_up * 5 // 13)
+    two = one + max(1, (n_up - one) // 2)
+    lag = min(LAG, n_up - one)
+    slot_rows = max(width, UNITS * max(one, two - one, n_up - two))
+    levels, before = [], 0
+    for first, last in ((0, one), (one, two), (two, n_up)):
+        most = min(4, slot_rows // ((last - first) * UNITS))
+        per = max(p for p in range(1, most + 1) if n_down % p == 0)
+        levels.append((first, last, per, n_down // per, before))
+        before += n_down // per
     all_rows = n_hid * rows
     bf16, f32 = jnp.bfloat16, jnp.float32
     dma = pltpu.SemaphoreType.DMA
     weights = 3 * width * hidden
     return pl.pallas_call(
-        functools.partial(kernel, n_hid, n_wid, keep, ring, lag),
+        functools.partial(kernel, n_hid, n_wid, keep, ring, lag, levels),
         out_shape=jax.ShapeDtypeStruct((rows, width), bf16),
         in_specs=[pl.BlockSpec(memory_space=pltpu.VMEM)]
         + [pl.BlockSpec(memory_space=pl.ANY)] * 3,
         out_specs=pl.BlockSpec(memory_space=pltpu.VMEM),
         scratch_shapes=[
-            pltpu.VMEM((keep + ring, max(width, hidden), 2 * UNITS), bf16),
+            pltpu.VMEM((keep + ring, slot_rows, 2 * UNITS), bf16),
             pltpu.VMEM((all_rows, width), f32),
             pltpu.VMEM((all_rows, width), bf16),
             pltpu.VMEM((STEPS, n_hid, n_down, TALL, LANES), bf16),
@@ -291,16 +371,17 @@
             pltpu.VMEM((STEPS, n_up, n_wid - 1, TALL, UNITS), bf16),
             pltpu.VMEM((STEPS, n_up, n_wid, TALL, LANES), bf16),
             pltpu.VMEM((all_rows, hidden), bf16),
+            pltpu.VMEM((n_down, all_rows, cols), f32),
             pltpu.VMEM((n_hid, TALL, LANES), f32),
             pltpu.VMEM((STEPS, n_down, n_hid, TALL, LANES), bf16),
             pltpu.VMEM((STEPS, n_down, n_hid - 1, TALL, LANES), bf16),
             pltpu.VMEM((n_down, TALL, LANES), f32),
             pltpu.VMEM((rows, width), f32),
-            dma((keep + ring, 2)),
+            dma((keep + ring, 4)),
             dma((STEPS, 2)),
             dma((STEPS,)),
             dma((STEPS, n_up)),
-            dma((STEPS, 2)),
+            dma((STEPS, len(levels) + 1)),
             dma((STEPS, 2)),
         ],
         compiler_params=pltpu.CompilerParams(
@@ -326,7 +407,7 @@
         and n_wid > 1
         and n_hid * rows == n_wid * (TALL // 2)
         and hidden % UNITS == 0
-        and hidden >= 2 * UNITS
+        and hidden >= 3 * UNITS
         and (TALL // rows) * LANES == 2 * UNITS
         and width % (2 * UNITS) == 0
     )

time: 77.2 us -> 75.3 us (0.975)
  Pallas kernels: 75.5 us -> 73.6 us
    pallas_call x1, Pallas kernels: 75.5 us -> 73.6 us  [fused(): pl.pallas_call(functools.partial(kernel, n_hid, n_wid, keep, ring, lag, l...]
where the time goes in v3:
time: 75.3 us; the launch traced here: 75 us
  Pallas kernels  73.6 us (98%)
  local copies, waits for them, and re-layouts  1.39 us (2%)
    pallas_call x1, Pallas kernels, fused(): pl.pallas_call(functools.partial(kernel, n_hid, n_wid, keep, ring, lag, l...  73.6 us

profile of v3, /device:TPU:0, one launch (start us, length us, event | category | flops | bytes accessed | tf_op | source)
XLA Modules:
  0.0 75.0 jit_solution(8949800039104000479)
XLA Ops:
  0.0 73.6 %shard_map.46 = bf16[4,4096]{1,0:T(4,128)(2,1)} custom-call(bf16[4,4096]{1,0:T(4,128)(2,1)} %tok_ref.1, bf16[4096,3328]{1,0:T(8,128)(2,1)} %gate_ref.1, bf16[4096,3328]{1,0:T(8,128)(2,1)} %up_ref.1, bf16[3328,4096]{1,0:T(8,128)(2,1)} %down_ref.1), custom_call_target="tpu_custom_call" | custom-call | flops 5234491392 | bytes 163577856 | tf_op jit(solution)/shard_map/pallas_call | solution.py:357
  73.6 1.4 %copy.6 = bf16[4,4096]{1,0:T(4,128)(2,1)} copy(bf16[4,4096]{1,0:T(4,128)(2,1)} %shard_map.46) | data formatting | bytes 65536

commit v4 on v3

--- a/solution.py
+++ b/solution.py
@@ -176,7 +176,19 @@
                     device_id_type=MESH,
                 ).start()
 
-        def piece(j, with_finish):
+        def send(j):
+            for d in range(1, n_wid):
+                peer = (wid + d) % n_wid
+                pltpu.make_async_remote_copy(
+                    src_ref=p_send.at[s, j, peer],
+                    dst_ref=p_got.at[s, j, d - 1],
+                    send_sem=p_send_sem.at[s],
+                    recv_sem=p_sem.at[s, j],
+                    device_id=(hid, peer),
+                    device_id_type=MESH,
+                ).start()
+
+        def piece(j, with_send, with_share, with_finish):
             q = s * streamed + j - keep
             kept = j < keep
             slot = jnp.where(kept, j, keep + (q + ring) % ring)
@@ -186,6 +198,10 @@
                 for copy in fetch_up(j, slot):
                     copy.wait()
 
+            if with_send:
+                send(j - 1)
+            if with_share:
+                share(j - 1 - lag)
             if with_finish:
                 landed(p_got.at[s, j - lag], p_sem.at[s, j - lag])
                 finish(j - lag)
@@ -197,30 +213,25 @@
                 p_send[s, j, w] = jnp.concatenate(
                     [product[lo:lo + group, :UNITS], product[lo:lo + group, UNITS:]], axis=0
                 ).astype(bf16)
-            for d in range(1, n_wid):
-                peer = (wid + d) % n_wid
-                pltpu.make_async_remote_copy(
-                    src_ref=p_send.at[s, j, peer],
-                    dst_ref=p_got.at[s, j, d - 1],
-                    send_sem=p_send_sem.at[s],
-                    recv_sem=p_sem.at[s, j],
-                    device_id=(hid, peer),
-                    device_id_type=MESH,
-                ).start()
-            if with_finish:
-                share(j - lag)
 
             @pl.when(jnp.logical_not(kept))
             def _():
                 start(q + ring)
 
-        @pl.loop(0, lag)
+        piece(0, False, False, False)
+
+        @pl.loop(1, lag)
         def _(j):
-            piece(j, False)
-
-        @pl.loop(lag, n_up)
+            piece(j, True, False, False)
+
+        piece(lag, True, False, True)
+
+        @pl.loop(lag + 1, n_up)
         def _(j):
-            piece(j, True)
+            piece(j, True, True, True)
+
+        send(n_up - 1)
+        share(n_up - 1 - lag)
 
         def gather_hidden(first, last, sem):
             landed(
@@ -250,13 +261,17 @@
                     branch[h, f * rows:(f + 1) * rows, :] = x_wide[
                         h * rows:(h + 1) * rows, f * LANES:(f + 1) * LANES
                     ]
-            d_send[s, c] = branch[...].astype(bf16)
+            for h in range(n_hid):
+                d_send[s, h, c] = branch[h].astype(bf16)
             d_own[c] = branch[hid]
+
+        def scatter(u, per):
+            part = pl.ds(per * u, per)
             for d in range(1, n_hid):
                 peer = (hid + d) % n_hid
                 pltpu.make_async_remote_copy(
-                    src_ref=d_send.at[s, c, peer],
-                    dst_ref=d_got.at[s, c, d - 1],
+                    src_ref=d_send.at[s, peer, part],
+                    dst_ref=d_got.at[s, d - 1, part],
                     send_sem=d_sems.at[s, 0],
                     recv_sem=d_sems.at[s, 1],
                     device_id=(peer, wid),
@@ -289,6 +304,8 @@
                 else:
                     x_wide[:, :cols] = partial[c] + term
                     spread(c)
+            if index == len(levels) - 1:
+                scatter(u, per)
             if finish_from is not None:
                 share(j)
             start(q + ring)
@@ -314,13 +331,13 @@
         landed(d_got.at[s], d_sems.at[s, 1])
         total = d_own[...]
         for d in range(n_hid - 1):
-            total = total + d_got[s, :, d].astype(f32)
+            total = total + d_got[s, d].astype(f32)
         own[...] = (own[...] + total).astype(bf16).astype(f32)
 
         landed(x_got.at[s, pl.ds(0, n_hid - 1)], x_sems.at[s, 0])
         landed(p_send.at[s, :, pl.ds(0, n_wid - 1)], p_send_sem.at[s])
         landed(h_got.at[s, :, pl.ds(0, n_wid - 1)], h_sems.at[s, len(levels)])
-        landed(d_send.at[s, :, pl.ds(0, n_hid - 1)], d_sems.at[s, 0])
+        landed(d_send.at[s, pl.ds(0, n_hid - 1)], d_sems.at[s, 0])
         return carry
 
     lax.fori_loop(0, STEPS, step, 0)
@@ -341,12 +358,12 @@
     keep = min(KEEP, n_up - 1)
     ring = RING
     one = max(1, n_up * 5 // 13)
-    two = one + max(1, (n_up - one) // 2)
+    two = one + max(1, (n_up - one) * 5 // 8)
     lag = min(LAG, n_up - one)
     slot_rows = max(width, UNITS * max(one, two - one, n_up - two))
     levels, before = [], 0
     for first, last in ((0, one), (one, two), (two, n_up)):
-        most = min(4, slot_rows // ((last - first) * UNITS))
+        most = min(2 if last == n_up else 4, slot_rows // ((last - first) * UNITS))
         per = max(p for p in range(1, most + 1) if n_down % p == 0)
         levels.append((first, last, per, n_down // per, before))
         before += n_down // per
@@ -373,8 +390,8 @@
             pltpu.VMEM((all_rows, hidden), bf16),
             pltpu.VMEM((n_down, all_rows, cols), f32),
             pltpu.VMEM((n_hid, TALL, LANES), f32),
-            pltpu.VMEM((STEPS, n_down, n_hid, TALL, LANES), bf16),
-            pltpu.VMEM((STEPS, n_down, n_hid - 1, TALL, LANES), bf16),
+            pltpu.VMEM((STEPS, n_hid, n_down, TALL, LANES), bf16),
+            pltpu.VMEM((STEPS, n_hid - 1, n_down, TALL, LANES), bf16),
             pltpu.VMEM((n_down, TALL, LANES), f32),
             pltpu.VMEM((rows, width), f32),
             dma((keep + ring, 4)),

time: 75.3 us -> 74.1 us (0.984)
  Pallas kernels: 73.6 us -> 72.5 us
    pallas_call x1, Pallas kernels: 73.6 us -> 72.5 us  [fused(): pl.pallas_call(functools.partial(kernel, n_hid, n_wid, keep, ring, lag, l...]
where the time goes in v4:
time: 74.1 us; the launch traced here: 73.9 us
  Pallas kernels  72.5 us (98%)
  local copies, waits for them, and re-layouts  1.39 us (2%)
    pallas_call x1, Pallas kernels, fused(): pl.pallas_call(functools.partial(kernel, n_hid, n_wid, keep, ring, lag, l...  72.5 us

profile of v4, /device:TPU:0, one launch (start us, length us, event | category | flops | bytes accessed | tf_op | source)
XLA Modules:
  0.0 73.9 jit_solution(9186766221344453042)
XLA Ops:
  0.0 72.5 %shard_map.46 = bf16[4,4096]{1,0:T(4,128)(2,1)} custom-call(bf16[4,4096]{1,0:T(4,128)(2,1)} %tok_ref.1, bf16[4096,3328]{1,0:T(8,128)(2,1)} %gate_ref.1, bf16[4096,3328]{1,0:T(8,128)(2,1)} %up_ref.1, bf16[3328,4096]{1,0:T(8,128)(2,1)} %down_ref.1), custom_call_target="tpu_custom_call" | custom-call | flops 5234491392 | bytes 163577856 | tf_op jit(solution)/shard_map/pallas_call | solution.py:374
  72.5 1.4 %copy.6 = bf16[4,4096]{1,0:T(4,128)(2,1)} copy(bf16[4,4096]{1,0:T(4,128)(2,1)} %shard_map.46) | data formatting | bytes 65536
